TPU v7x, 32 devices: a whole 2x2x4 slice. The times are simulated.
32 devices in a mesh: parts: 2 (over y), grid: 16 (over z, x, core).
Axes of the slice: x: 2, y: 2, z: 4, core: 2. Of those that a mesh axis runs over, the one named last changes fastest.
Arguments:
- observations: float32 [2048, 40, 1024], P(('parts', 'grid')), parts along dimension 0, may hold values from -16 to 16
- observation_mask: int32 [2048, 40, 1024], P(('parts', 'grid')), parts along dimension 0, may hold values 0 or 1
- noise_class: int32 [2048], P(('parts', 'grid')), parts along dimension 0, may hold values from 0 to 3
- station_kernel: bfloat16 [1024, 1024], replicated, may hold values from -1 to 2, as said below
- time_kernel: bfloat16 [1024, 1024], replicated, may hold values from -1 to 2, as said below
- variable_cov: bfloat16 [40, 40], replicated, may hold values from -1 to 2, as said below
Outputs:
- solution: float32 [2048, 40, 1024], P(('parts', 'grid')), parts along dimension 0
- residual: float32 [2048, 40, 1024], P(('parts', 'grid')), parts along dimension 0
There are 2 independent parts, one for each index of `parts`. A program takes and returns all parts, laid end to end along the dimension named above; an argument that names none is the same for every part. Nothing has to cross between parts.
Inputs may be any that keep to these rules, and one draw needn't show every extreme that they name: `station_kernel`: symmetric. `time_kernel`: symmetric. `variable_cov`: symmetric.
All inputs are finite; a program needn't handle non-finite values. No bound on the sum of `observation_mask` on one device may be relied on, other than what follows from the above.
Results may differ from a plain program's by a relative error of at most 0.0094.
Values may be sent and summed in bfloat16 or wider, within the bound.
A program may use at most 192 MiB of HBM per device.

v0:
```python
import jax
import jax.numpy as jnp
from jax import lax
from jax.sharding import PartitionSpec as P

ITERS = 2


noise_levels = (0.05, 0.2, 0.6, 1.5)


def body(observations, observation_mask, noise_class, station_kernel, time_kernel, variable_cov):
    devices = lax.axis_size("grid")
    stations, variables, length = observations.shape
    block = length // devices
    groups = 2
    per_group = variables // groups
    levels = jnp.zeros((stations,), jnp.float32)
    for level_index, level_value in enumerate(noise_levels):
        levels = levels + jnp.where(noise_class == level_index, level_value, 0.0)
    noise_cells = levels[:, None, None]
    mask_float = observation_mask.astype(jnp.float32)
    time_blocks = time_kernel.reshape(devices, block, length)
    target = mask_float * observations
    solution = jnp.zeros_like(target)
    residual = target
    for inner_index in range(ITERS):
        norm_sq = lax.psum(jnp.sum(residual * residual), "grid")
        rounded = residual.astype(jnp.bfloat16)
        mixed = jnp.einsum(
            "wv,svt->swt", variable_cov, rounded, preferred_element_type=jnp.float32
        ).astype(jnp.bfloat16)
        grouped = mixed.reshape(stations, groups, per_group, length)
        timed = jnp.einsum(
            "sgwt,dbt->sdgbw", grouped, time_blocks, preferred_element_type=jnp.float32
        ).astype(jnp.bfloat16)
        pieces = timed.reshape(stations, devices, groups, block * per_group)
        operator_gathered = lax.all_to_all(pieces, "grid", split_axis=1, concat_axis=0, tiled=True)
        spaced = lax.all_to_all(
            jnp.einsum(
                "rs,sdgk->rdgk",
                station_kernel,
                operator_gathered,
                preferred_element_type=jnp.float32,
            ).astype(jnp.bfloat16),
            "grid",
            split_axis=0,
            concat_axis=1,
            tiled=True,
        )
        spaced = spaced.reshape(stations, devices, groups, block, per_group)
        spaced = (
            jnp.transpose(spaced, (0, 2, 4, 1, 3))
            .reshape(stations, variables, length)
            .astype(jnp.float32)
        )
        image = mask_float * spaced + noise_cells * residual
        curvature = lax.psum(jnp.sum(residual * image), "grid")
        step_size = norm_sq / curvature
        solution, residual = (solution + step_size * residual, residual - step_size * image)
    return (solution, residual)


def solution(mesh):
    return jax.shard_map(
        body,
        mesh=mesh,
        in_specs=(
            P(("parts", "grid"), None, None),
            P(("parts", "grid"), None, None),
            P(("parts", "grid")),
            P(),
            P(),
            P(),
        ),
        out_specs=(P(("parts", "grid"), None, None), P(("parts", "grid"), None, None)),
        check_vma=False,
    )
```

profile of v0, /device:TPU:0, one launch (start us, length us, event | category | flops | bytes accessed | tf_op | source)
XLA Modules:
  0.0 897.4 jit_solution(10119833041073293713)
XLA Ops:
  0.6 0.0 copy-start
  0.6 0.0 copy-start.3
  0.7 15.1 %convert_multiply_fusion.2 = f32[64,40,1024]{2,1,0:T(8,128)} fusion(f32[64,40,1024]{2,1,0:T(8,128)} %param.6, s32[64,40,1024]{2,1,0:T(8,128)} %param.7), kind=kLoop, calls=%fused_computation.15 | loop fusion | flops 5242880 | bytes 31457280 | tf_op jit(solution)/shard_map/mul | solution.py:24
  15.7 0.0 copy-done.3
  15.7 5.8 convert_bitcast_fusion.5
  21.5 2.9 copy.50
  24.4 0.0 copy-done
  24.4 13.2 %convert_bitcast_fusion.3 = bf16[64,16,2,64,20]{3,0,1,4,2:T(8,128)(2,1)} fusion(bf16[64,2,20,1024,1]{3,0,4,2,1:T(8,128)(2,1)S(1)} %bitcast.85, bf16[16,64,1024,1,1]{2,1,0,4,3:T(8,128)(2,1)S(1)} %bitcast.77), kind=kOutput, calls=%fused_computation.11 | convolution fusion | flops 5371330560 | bytes 12582912 | tf_op jit(solution)/shard_map/sgwt,dbt->sdgbw/dot_general | solution.py:34
  37.6 15.4 %copy.51 = bf16[64,16,2,64,20]{0,1,4,3,2:T(8,128)(2,1)} copy(bf16[64,16,2,64,20]{3,0,1,4,2:T(8,128)(2,1)} %convert_bitcast_fusion.3) | data formatting | bytes 10485760 | tf_op jit(solution)/shard_map/convert_element_type | solution.py:36
  53.0 11.9 %copy.52 = bf16[64,16,2,1280]{3,0,2,1:T(8,128)(2,1)} copy(bf16[64,16,2,1280]{0,1,3,2:T(8,128)(2,1)} %bitcast.81) | data formatting | bytes 10485760 | tf_op jit(solution)/shard_map/reshape | solution.py:37
  64.9 122.4 %all_to_all.54 = bf16[64,16,2,1280]{3,0,2,1:T(8,128)(2,1)S(1)} all-to-all(bf16[64,16,2,1280]{3,0,2,1:T(8,128)(2,1)} %copy.52), channel_id=1, replica_groups=mesh['parts'=2,'grid'=16] {'grid'}, dimensions={1} | all-to-all | bytes 10485760 | tf_op jit(solution)/shard_map/all_to_all | solution.py:38
  187.3 0.6 copy.53
  187.9 0.0 copy-done.4
  187.9 7.4 fusion.4
  195.3 13.8 %copy.55 = bf16[1024,1,2,1280]{3,2,1,0:T(2,128)(2,1)} copy(bf16[1024,1,2,1280]{0,3,2,1:T(8,128)(2,1)} %fusion.4) | data formatting | bytes 10485760 | tf_op jit(solution)/shard_map/convert_element_type | solution.py:45
  209.1 5.4 all-to-all-start.1
  214.5 0.0 copy-done.6
  214.5 95.9 %all-to-all-done.1 = bf16[1024,1,2,1280]{3,2,1,0:T(2,128)(2,1)} async-done(((bf16[1024,1,2,1280]{3,2,1,0:T(2,128)(2,1)}), bf16[1024,1,2,1280]{3,2,1,0:T(2,128)(2,1)}, u32[]{:S(2)}, u32[]{:S(2)}) %all-to-all-start.1) | async-done | bytes 5242912 | tf_op jit(solution)/shard_map/all_to_all | solution.py:39
  310.4 3.1 copy.56
  313.6 5.4 convert_bitcast_fusion.1
  319.0 17.7 %copy.57 = f32[64,16,1,2,1280]{0,1,4,3,2:T(8,128)} copy(f32[64,16,1,2,1280]{4,0,1,3,2:T(8,128)} %convert_bitcast_fusion.1) | data formatting | bytes 20971520 | tf_op jit(solution)/shard_map/convert_element_type | solution.py:55
  336.7 22.5 %copy.58 = f32[64,2,20,16,64]{4,3,2,1,0:T(8,128)} copy(f32[64,2,20,16,64]{0,3,2,4,1:T(8,128)} %bitcast.79) | data formatting | bytes 20971520 | tf_op jit(solution)/shard_map/convert_element_type | solution.py:55
  359.1 18.1 %reshape.53 = f32[64,40,1024]{2,1,0:T(8,128)} reshape(f32[64,2,20,16,64]{4,3,2,1,0:T(8,128)} %copy.58) | data formatting | bytes 20971520 | tf_op jit(solution)/shard_map/convert_element_type | solution.py:55
  377.3 12.4 %multiply_reduce_fusion.2 = (f32[]{:T(128)}, f32[]{:T(128)}) fusion(f32[64,40,1024]{2,1,0:T(8,128)} %convert_multiply_fusion.2, f32[64]{0:T(128)S(1)} %fusion.16, f32[64,40,1024]{2,1,0:T(8,128)} %reshape.53, s32[64,40,1024]{2,1,0:T(8,128)} %param.7), kind=kLoop, calls=%fused_computation.9 | loop fusion | flops 20971520 | bytes 31457544 | tf_op jit(solution)/shard_map/reduce_sum | solution.py:58
  389.7 52.7 %all-reduce.1 = (f32[]{:T(128)}, f32[]{:T(128)}) all-reduce(f32[]{:T(128)} %get-tuple-element.5, f32[]{:T(128)} %get-tuple-element.4), channel_id=1, replica_groups=mesh['parts'=2,'grid'=16] {'grid'}, use_global_device_ids=true, to_apply=%region_1.2 | all-reduce | flops 2 | bytes 16 | tf_op jit(solution)/shard_map/psum | solution.py:28
  443.8 11.6 %multiply_subtract_fusion.1 = f32[64,40,1024]{2,1,0:T(8,128)S(1)} fusion(f32[64,40,1024]{2,1,0:T(8,128)} %convert_multiply_fusion.2, f32[]{:T(128)S(6)} %div.6, f32[64]{0:T(128)S(1)} %fusion.16, f32[64,40,1024]{2,1,0:T(8,128)} %reshape.53, s32[64,40,1024]{2,1,0:T(8,128)} %param.7), kind=kLoop, calls=%fused_computation.8 | loop fusion | flops 15728640 | bytes 41943300 | tf_op jit(solution)/shard_map/sub | solution.py:60
  455.4 0.0 copy-start.2
  455.4 1.8 convert_bitcast_fusion.4
  457.2 2.9 copy.59
  460.1 0.0 copy-done.2
  460.1 13.2 %convert_bitcast_fusion.2 = bf16[64,16,2,64,20]{3,0,1,4,2:T(8,128)(2,1)} fusion(bf16[64,2,20,1024,1]{3,0,4,2,1:T(8,128)(2,1)S(1)} %bitcast.87, bf16[16,64,1024,1,1]{2,1,0,4,3:T(8,128)(2,1)S(1)} %bitcast.78), kind=kOutput, calls=%fused_computation.6 | convolution fusion | flops 5371330560 | bytes 12582912 | tf_op jit(solution)/shard_map/sgwt,dbt->sdgbw/dot_general | solution.py:34
  473.3 15.4 %copy.60 = bf16[64,16,2,64,20]{0,1,4,3,2:T(8,128)(2,1)} copy(bf16[64,16,2,64,20]{3,0,1,4,2:T(8,128)(2,1)} %convert_bitcast_fusion.2) | data formatting | bytes 10485760 | tf_op jit(solution)/shard_map/convert_element_type | solution.py:36
  488.7 12.0 %copy.61 = bf16[64,16,2,1280]{3,0,2,1:T(8,128)(2,1)} copy(bf16[64,16,2,1280]{0,1,3,2:T(8,128)(2,1)} %bitcast.82) | data formatting | bytes 10485760 | tf_op jit(solution)/shard_map/reshape | solution.py:37
  500.7 118.8 %all_to_all.55 = bf16[64,16,2,1280]{3,0,2,1:T(8,128)(2,1)S(1)} all-to-all(bf16[64,16,2,1280]{3,0,2,1:T(8,128)(2,1)} %copy.61), channel_id=1, replica_groups=mesh['parts'=2,'grid'=16] {'grid'}, dimensions={1} | all-to-all | bytes 10485760 | tf_op jit(solution)/shard_map/all_to_all | solution.py:38
  619.5 0.6 copy.62
  620.0 0.0 copy-done.5
  620.1 7.5 fusion.5
  627.5 13.8 %copy.64 = bf16[1024,1,2,1280]{3,2,1,0:T(2,128)(2,1)} copy(bf16[1024,1,2,1280]{0,3,2,1:T(8,128)(2,1)} %fusion.5) | data formatting | bytes 10485760 | tf_op jit(solution)/shard_map/convert_element_type | solution.py:45
  641.3 119.7 %all_to_all.56 = bf16[1024,1,2,1280]{3,2,1,0:T(2,128)(2,1)S(1)} all-to-all(bf16[1024,1,2,1280]{3,2,1,0:T(2,128)(2,1)} %copy.64), channel_id=1, replica_groups=mesh['parts'=2,'grid'=16] {'grid'}, dimensions={0} | all-to-all | bytes 10485760 | tf_op jit(solution)/shard_map/all_to_all | solution.py:39
  761.0 0.7 copy.65
  761.6 5.3 convert_bitcast_fusion
  766.9 17.7 %copy.66 = f32[64,16,1,2,1280]{0,1,4,3,2:T(8,128)} copy(f32[64,16,1,2,1280]{4,0,1,3,2:T(8,128)} %convert_bitcast_fusion) | data formatting | bytes 20971520 | tf_op jit(solution)/shard_map/convert_element_type | solution.py:55
  784.6 22.5 %copy.67 = f32[64,2,20,16,64]{4,3,2,1,0:T(8,128)} copy(f32[64,2,20,16,64]{0,3,2,4,1:T(8,128)} %bitcast.80) | data formatting | bytes 20971520 | tf_op jit(solution)/shard_map/convert_element_type | solution.py:55
  807.1 18.1 %reshape.54 = f32[64,40,1024]{2,1,0:T(8,128)} reshape(f32[64,2,20,16,64]{4,3,2,1,0:T(8,128)} %copy.67) | data formatting | bytes 20971520 | tf_op jit(solution)/shard_map/convert_element_type | solution.py:55
  825.2 12.4 %multiply_reduce_fusion = (f32[]{:T(128)}, f32[]{:T(128)}) fusion(f32[64,40,1024]{2,1,0:T(8,128)} %copy-done.2, f32[64]{0:T(128)S(1)} %fusion.16, f32[64,40,1024]{2,1,0:T(8,128)} %reshape.54, s32[64,40,1024]{2,1,0:T(8,128)} %param.7), kind=kLoop, calls=%fused_computation.4 | loop fusion | flops 20971520 | bytes 31457544 | tf_op jit(solution)/shard_map/reduce_sum | solution.py:58
  837.6 34.1 %all-reduce = (f32[]{:T(128)}, f32[]{:T(128)}) all-reduce(f32[]{:T(128)} %get-tuple-element.3, f32[]{:T(128)} %get-tuple-element.2), channel_id=1, replica_groups=mesh['parts'=2,'grid'=16] {'grid'}, use_global_device_ids=true, to_apply=%region_5.6 | all-reduce | flops 2 | bytes 16 | tf_op jit(solution)/shard_map/psum | solution.py:28
  873.0 0.0 copy-start.1
  873.0 23.9 %multiply_subtract_fusion = (f32[64,40,1024]{2,1,0:T(8,128)}, f32[64,40,1024]{2,1,0:T(8,128)}) fusion(f32[64,40,1024]{2,1,0:T(8,128)} %copy-done.2, f32[]{:T(128)S(6)} %div.7, f32[64]{0:T(128)S(1)} %fusion.16, f32[64,40,1024]{2,1,0:T(8,128)} %reshape.54, s32[64,40,1024]{2,1,0:T(8,128)} %param.7, f32[64,40,1024]{2,1,0:T(8,128)} %convert_multiply_fusion.2, ...), kind=kLoop, calls=%fused_computation.2 | loop fusion | flops 23592960 | bytes 62914824 | tf_op jit(solution)/shard_map/sub | solution.py:60
  (5 shorter events, 0.0 us)
Async XLA Ops:
  0.6 23.8 %copy-start = (bf16[1024,1024]{1,0:T(8,128)(2,1)S(1)}, bf16[1024,1024]{1,0:T(8,128)(2,1)}, u32[]{:S(2)}) copy-start(bf16[1024,1024]{1,0:T(8,128)(2,1)} %param.10) | copy-start | bytes 6291460
  0.6 15.1 %copy-start.3 = (bf16[40,40]{1,0:T(8,128)(2,1)S(1)}, bf16[40,40]{1,0:T(8,128)(2,1)}, u32[]{:S(2)}) copy-start(bf16[40,40]{1,0:T(8,128)(2,1)} %param.11) | copy-start | bytes 9604
  64.9 123.0 %copy-start.4 = (bf16[1024,1024]{1,0:T(8,128)(2,1)S(1)}, bf16[1024,1024]{1,0:T(8,128)(2,1)}, u32[]{:S(2)}) copy-start(bf16[1024,1024]{1,0:T(8,128)(2,1)} %param.9) | copy-start | bytes 6291460
  195.3 19.2 %copy-start.6 = (s32[64]{0:T(128)S(1)}, s32[64]{0:T(128)}, u32[]{:S(2)}) copy-start(s32[64]{0:T(128)} %param.8) | copy-start | bytes 772
  209.1 101.3 %all-to-all-start.1 = ((bf16[1024,1,2,1280]{3,2,1,0:T(2,128)(2,1)}), bf16[1024,1,2,1280]{3,2,1,0:T(2,128)(2,1)}, u32[]{:S(2)}, u32[]{:S(2)}) async-start(bf16[1024,1,2,1280]{3,2,1,0:T(2,128)(2,1)} %copy.55), calls=%async_computation.1 | async-start | bytes 10485760 | tf_op jit(solution)/shard_map/all_to_all | solution.py:39
  455.4 4.7 copy-start.2
  500.7 119.4 %copy-start.5 = (bf16[1024,1024]{1,0:T(8,128)(2,1)S(1)}, bf16[1024,1024]{1,0:T(8,128)(2,1)}, u32[]{:S(2)}) copy-start(bf16[1024,1024]{1,0:T(8,128)(2,1)} %param.9) | copy-start | bytes 6291460
  873.0 23.9 %copy-start.1 = (bf16[1024,1024]{1,0:T(8,128)(2,1)S(1)}, bf16[1024,1024]{1,0:T(8,128)(2,1)}, u32[]{:S(2)}) copy-start(bf16[1024,1024]{1,0:T(8,128)(2,1)} %param.10) | copy-start | bytes 6291460
where the time goes:
time: 910 us; the launch traced here: 897 us
  blocking collectives  448 us (49%)
  local copies, waits for them, and re-layouts  210 us (23%)
  waiting for transfers between devices  95.9 us (11%)
  other arithmetic  86.1 us (9%)
  matrix products  48.8 us (5%)
    all_to_all x2, blocking collectives, body(): lax.all_to_all(pieces, 'grid', split_axis=1, concat_axis=0, tiled=True)  241 us
    all_to_all x1, blocking collectives, body(): lax.all_to_all(jnp.einsum('rs,sdgk->rdgk', station_kernel, operator_gathe...  120 us
    convert_element_type x6, local copies, waits for them, and re-layouts, body(): spaced = jnp.transpose(spaced, (0, 2, 4, 1, 3)).reshape(stations, variabl...  117 us
    all_to_all x1, waiting for transfers between devices, body(): lax.all_to_all(jnp.einsum('rs,sdgk->rdgk', station_kernel, operator_gathe...  95.9 us
    psum x2, blocking collectives, body(): norm_sq = lax.psum(jnp.sum(residual * residual), 'grid')  86.8 us
    sub x2, other arithmetic, body(): residual - step_size * image  35.6 us
    convert_element_type x2, local copies, waits for them, and re-layouts, body(): timed = jnp.einsum('sgwt,dbt->sdgbw', grouped, time_blocks, preferred_ele...  30.8 us
    convert_element_type x2, local copies, waits for them, and re-layouts, body(): spaced = lax.all_to_all(jnp.einsum('rs,sdgk->rdgk', station_kernel, opera...  27.5 us
  transfers between devices with their start and end apart: 1, of which 1 were waited for; matrix products, arithmetic and copies ran while one was open for 0% of the time, Pallas kernels for 0%

commit v1 on v0

v1 whole, which is shorter than its diff:
```python
import math

import jax
import jax.numpy as jnp
from jax import lax
from jax.sharding import PartitionSpec as P

ITERS = 2


noise_levels = (0.05, 0.2, 0.6, 1.5)


def body(observations, observation_mask, noise_class, station_kernel, time_kernel, variable_cov):
    devices = lax.axis_size("grid")
    stations, variables, length = observations.shape
    all_stations = station_kernel.shape[0]
    columns = variables * length // devices
    lane = math.gcd(math.gcd(128, columns), length)
    tiles = length // lane
    chunk = columns // lane
    levels = jnp.zeros((stations,), jnp.float32)
    for level_index, level_value in enumerate(noise_levels):
        levels = levels + jnp.where(noise_class == level_index, level_value, 0.0)
    noise_cells = levels[:, None, None]
    mask_float = observation_mask.astype(jnp.float32)
    target = mask_float * observations
    solution = jnp.zeros_like(target)
    residual = target
    for inner_index in range(ITERS):
        rounded = residual.astype(jnp.bfloat16)
        mixed = jnp.einsum(
            "wv,svt->swt", variable_cov, rounded, preferred_element_type=jnp.float32
        ).astype(jnp.bfloat16)
        timed = jnp.einsum(
            "wst,ut->wsu", jnp.transpose(mixed, (1, 0, 2)), time_kernel, preferred_element_type=jnp.float32
        ).astype(jnp.bfloat16)
        pieces = timed.reshape(variables, stations, tiles, lane)
        pieces = jnp.transpose(pieces, (0, 2, 1, 3)).reshape(devices, chunk, stations, lane)
        gathered = lax.all_to_all(pieces, "grid", split_axis=0, concat_axis=0, tiled=True)
        gathered = jnp.transpose(gathered, (0, 2, 1, 3)).reshape(all_stations, chunk * lane)
        spaced = jnp.einsum(
            "rs,sk->rk", station_kernel, gathered, preferred_element_type=jnp.float32
        ).astype(jnp.bfloat16)
        spaced = jnp.transpose(spaced.reshape(devices, stations, chunk, lane), (0, 2, 1, 3))
        spaced = lax.all_to_all(spaced, "grid", split_axis=0, concat_axis=0, tiled=True)
        spaced = jnp.transpose(spaced.reshape(variables, tiles, stations, lane), (2, 0, 1, 3))
        spaced = spaced.reshape(stations, variables, length).astype(jnp.float32)
        image = mask_float * spaced + noise_cells * residual
        norm_sq, curvature = lax.psum((jnp.sum(residual * residual), jnp.sum(residual * image)), "grid")
        step_size = norm_sq / curvature
        solution, residual = (solution + step_size * residual, residual - step_size * image)
    return (solution, residual)


def solution(mesh):
    return jax.shard_map(
        body,
        mesh=mesh,
        in_specs=(
            P(("parts", "grid"), None, None),
            P(("parts", "grid"), None, None),
            P(("parts", "grid")),
            P(),
            P(),
            P(),
        ),
        out_specs=(P(("parts", "grid"), None, None), P(("parts", "grid"), None, None)),
        check_vma=False,
    )
```

time: 910 us -> 780 us (0.86)
  local copies, waits for them, and re-layouts: 210 us -> 101 us
  matrix products: 48.8 us -> 35.3 us
    convert_element_type x12 -> x6, local copies, waits for them, and re-layouts: 181 us -> 58.8 us  [the longest x4 43.1 us: body(): spaced = spaced.reshape(stations, variables, length).astype(jnp.float32)]
    transpose x0 -> x4, local copies, waits for them, and re-layouts: none -> 19.8 us  [the longest x2 11 us: body(): jnp.transpose(spaced.reshape(devices, stations, chunk, lane), (0, 2, 1, 3))]
    dot_general x4, matrix products: 41.2 us -> 27.7 us  [the longest x2 14.9 us: body(): jnp.einsum('rs,sk->rk', station_kernel, gathered, preferred_element_type=...]
    reshape x2 -> x4, local copies, waits for them, and re-layouts: 23.9 us -> 22.8 us  [the longest x2 19.9 us: body(): spaced.reshape(devices, stations, chunk, lane)]
where the time goes in v1:
time: 780 us; the launch traced here: 772 us
  blocking collectives  447 us (57%)
  local copies, waits for them, and re-layouts  101 us (13%)
  waiting for transfers between devices  95.9 us (12%)
  other arithmetic  83.1 us (11%)
  matrix products  35.3 us (5%)
    all_to_all x2, blocking collectives, body(): lax.all_to_all(pieces, 'grid', split_axis=0, concat_axis=0, tiled=True)  240 us
    all_to_all x1, blocking collectives, body(): lax.all_to_all(spaced, 'grid', split_axis=0, concat_axis=0, tiled=True)  120 us
    all_to_all x1, waiting for transfers between devices, body(): lax.all_to_all(spaced, 'grid', split_axis=0, concat_axis=0, tiled=True)  95.9 us
    psum x2, blocking collectives, body(): lax.psum((jnp.sum(residual * residual), jnp.sum(residual * image)), 'grid')  86.7 us
    convert_element_type x4, local copies, waits for them, and re-layouts, body(): spaced = spaced.reshape(stations, variables, length).astype(jnp.float32)  43.1 us
    sub x2, other arithmetic, body(): residual - step_size * image  35.6 us
    reduce_sum x2, other arithmetic, body(): jnp.sum(residual * image)  24.8 us
    reshape x2, local copies, waits for them, and re-layouts, body(): spaced.reshape(devices, stations, chunk, lane)  19.9 us
  transfers between devices with their start and end apart: 1, of which 1 were waited for; matrix products, arithmetic and copies ran while one was open for 0% of the time, Pallas kernels for 0%

profile of v1, /device:TPU:0, one launch (start us, length us, event | category | flops | bytes accessed | tf_op | source)
XLA Modules:
  0.0 771.7 jit_solution(16345484615124459292)
XLA Ops:
  0.6 0.0 copy-start
  0.6 0.0 copy-start.3
  0.7 15.1 %convert_multiply_fusion.2 = f32[64,40,1024]{2,1,0:T(8,128)} fusion(f32[64,40,1024]{2,1,0:T(8,128)} %param.6, s32[64,40,1024]{2,1,0:T(8,128)} %param.7), kind=kLoop, calls=%fused_computation.13 | loop fusion | flops 5242880 | bytes 31457280 | tf_op jit(solution)/shard_map/mul | solution.py:27
  15.7 0.0 copy-done.3
  15.7 5.8 convert_bitcast_fusion.5
  21.5 0.0 copy-done
  21.5 6.4 convert_bitcast_fusion.4
  27.9 1.5 copy.67
  29.4 0.0 copy-start.4
  29.4 122.5 %all_to_all.20 = bf16[16,20,64,128]{3,2,1,0:T(8,128)(2,1)S(1)} all-to-all(bf16[16,20,64,128]{3,2,1,0:T(8,128)(2,1)S(1)} %bitcast.68), channel_id=1, replica_groups=mesh['parts'=2,'grid'=16] {'grid'}, dimensions={0} | all-to-all | bytes 10485760 | tf_op jit(solution)/shard_map/all_to_all | solution.py:40
  151.9 4.4 copy.30
  156.3 0.0 copy-done.4
  156.3 7.4 fusion.12
  163.7 7.8 %copy.31 = bf16[1024,2560]{1,0:T(8,128)(2,1)} copy(bf16[1024,2560]{0,1:T(8,128)(2,1)} %fusion.12) | data formatting | bytes 10485760 | tf_op jit(solution)/shard_map/convert_element_type | solution.py:44
  171.5 10.0 %reshape.44 = bf16[16,64,20,128]{3,2,1,0:T(8,128)(2,1)} reshape(bf16[1024,2560]{1,0:T(8,128)(2,1)} %copy.31) | data formatting | bytes 10485760 | tf_op jit(solution)/shard_map/reshape | solution.py:45
  181.5 0.0 copy-start.6
  181.5 6.7 copy.32
  188.1 5.6 all-to-all-start.1
  193.8 0.0 copy-done.6
  193.8 95.9 %all-to-all-done.1 = bf16[16,20,64,128]{3,2,1,0:T(8,128)(2,1)} async-done(((bf16[16,20,64,128]{3,2,1,0:T(8,128)(2,1)}), bf16[16,20,64,128]{3,2,1,0:T(8,128)(2,1)}, u32[]{:S(2)}, u32[]{:S(2)}) %all-to-all-start.1) | async-done | bytes 5242912 | tf_op jit(solution)/shard_map/all_to_all | solution.py:46
  289.7 3.8 convert_bitcast_fusion.1
  293.5 10.2 %copy.33 = f32[64,40,8,128]{3,2,1,0:T(8,128)} copy(f32[64,40,8,128]{3,0,2,1:T(8,128)S(1)} %convert_bitcast_fusion.1) | data formatting | bytes 20971520 | tf_op jit(solution)/shard_map/convert_element_type | solution.py:48
  303.7 11.5 %reshape.49 = f32[64,40,1024]{2,1,0:T(8,128)} reshape(f32[64,40,8,128]{3,2,1,0:T(8,128)} %copy.33) | data formatting | bytes 20971520 | tf_op jit(solution)/shard_map/convert_element_type | solution.py:48
  315.2 12.4 %multiply_reduce_fusion.2 = (f32[]{:T(128)}, f32[]{:T(128)}) fusion(f32[64,40,1024]{2,1,0:T(8,128)} %convert_multiply_fusion.2, f32[64]{0:T(128)S(1)} %fusion.32, f32[64,40,1024]{2,1,0:T(8,128)} %reshape.49, s32[64,40,1024]{2,1,0:T(8,128)} %param.7), kind=kLoop, calls=%fused_computation.8 | loop fusion | flops 20971520 | bytes 31457544 | tf_op jit(solution)/shard_map/reduce_sum | solution.py:50
  327.6 52.7 %all-reduce.1 = (f32[]{:T(128)}, f32[]{:T(128)}) all-reduce(f32[]{:T(128)} %get-tuple-element.5, f32[]{:T(128)} %get-tuple-element.4), channel_id=1, replica_groups=mesh['parts'=2,'grid'=16] {'grid'}, use_global_device_ids=true, to_apply=%region_1.2 | all-reduce | flops 2 | bytes 16 | tf_op jit(solution)/shard_map/psum | solution.py:50
  381.5 11.6 %multiply_subtract_fusion.1 = f32[64,40,1024]{2,1,0:T(8,128)S(1)} fusion(f32[64,40,1024]{2,1,0:T(8,128)} %convert_multiply_fusion.2, f32[]{:T(128)S(6)} %div.6, f32[64]{0:T(128)S(1)} %fusion.32, f32[64,40,1024]{2,1,0:T(8,128)} %reshape.49, s32[64,40,1024]{2,1,0:T(8,128)} %param.7), kind=kLoop, calls=%fused_computation.7 | loop fusion | flops 15728640 | bytes 41943300 | tf_op jit(solution)/shard_map/sub | solution.py:52
  393.1 0.0 copy-start.2
  393.1 1.8 convert_bitcast_fusion.3
  395.0 6.4 convert_bitcast_fusion.2
  401.4 0.0 copy-done.2
  401.4 1.5 copy.66
  402.9 0.0 copy-start.5
  402.9 117.9 %all_to_all.21 = bf16[16,20,64,128]{3,2,1,0:T(8,128)(2,1)S(1)} all-to-all(bf16[16,20,64,128]{3,2,1,0:T(8,128)(2,1)S(1)} %bitcast.70), channel_id=1, replica_groups=mesh['parts'=2,'grid'=16] {'grid'}, dimensions={0} | all-to-all | bytes 10485760 | tf_op jit(solution)/shard_map/all_to_all | solution.py:40
  520.8 4.4 copy.36
  525.2 0.0 copy-done.5
  525.2 7.5 fusion.15
  532.6 7.9 %copy.37 = bf16[1024,2560]{1,0:T(8,128)(2,1)} copy(bf16[1024,2560]{0,1:T(8,128)(2,1)} %fusion.15) | data formatting | bytes 10485760 | tf_op jit(solution)/shard_map/convert_element_type | solution.py:44
  540.6 10.0 %reshape.48 = bf16[16,64,20,128]{3,2,1,0:T(8,128)(2,1)} reshape(bf16[1024,2560]{1,0:T(8,128)(2,1)} %copy.37) | data formatting | bytes 10485760 | tf_op jit(solution)/shard_map/reshape | solution.py:45
  550.5 4.3 copy.38
  554.8 119.8 %all_to_all.22 = bf16[16,20,64,128]{3,2,1,0:T(8,128)(2,1)} all-to-all(bf16[16,20,64,128]{3,2,1,0:T(8,128)(2,1)S(1)} %copy.38), channel_id=1, replica_groups=mesh['parts'=2,'grid'=16] {'grid'}, dimensions={0} | all-to-all | bytes 10485760 | tf_op jit(solution)/shard_map/all_to_all | solution.py:46
  674.6 3.8 convert_bitcast_fusion
  678.4 9.9 %copy.39 = f32[64,40,8,128]{3,2,1,0:T(8,128)} copy(f32[64,40,8,128]{3,0,2,1:T(8,128)S(1)} %convert_bitcast_fusion) | data formatting | bytes 20971520 | tf_op jit(solution)/shard_map/convert_element_type | solution.py:48
  688.3 11.5 %reshape.50 = f32[64,40,1024]{2,1,0:T(8,128)} reshape(f32[64,40,8,128]{3,2,1,0:T(8,128)} %copy.39) | data formatting | bytes 20971520 | tf_op jit(solution)/shard_map/convert_element_type | solution.py:48
  699.8 12.4 %multiply_reduce_fusion = (f32[]{:T(128)}, f32[]{:T(128)}) fusion(f32[64,40,1024]{2,1,0:T(8,128)} %copy-done.2, f32[64]{0:T(128)S(1)} %fusion.32, f32[64,40,1024]{2,1,0:T(8,128)} %reshape.50, s32[64,40,1024]{2,1,0:T(8,128)} %param.7), kind=kLoop, calls=%fused_computation.4 | loop fusion | flops 20971520 | bytes 31457544 | tf_op jit(solution)/shard_map/reduce_sum | solution.py:50
  712.2 34.0 %all-reduce = (f32[]{:T(128)}, f32[]{:T(128)}) all-reduce(f32[]{:T(128)} %get-tuple-element.3, f32[]{:T(128)} %get-tuple-element.2), channel_id=1, replica_groups=mesh['parts'=2,'grid'=16] {'grid'}, use_global_device_ids=true, to_apply=%region_5.6 | all-reduce | flops 2 | bytes 16 | tf_op jit(solution)/shard_map/psum | solution.py:50
  747.6 0.0 copy-start.1
  747.6 23.9 %multiply_subtract_fusion = (f32[64,40,1024]{2,1,0:T(8,128)}, f32[64,40,1024]{2,1,0:T(8,128)}) fusion(f32[64,40,1024]{2,1,0:T(8,128)} %copy-done.2, f32[]{:T(128)S(6)} %div.7, f32[64]{0:T(128)S(1)} %fusion.32, f32[64,40,1024]{2,1,0:T(8,128)} %reshape.50, s32[64,40,1024]{2,1,0:T(8,128)} %param.7, f32[64,40,1024]{2,1,0:T(8,128)} %convert_multiply_fusion.2, ...), kind=kLoop, calls=%fused_computation.2 | loop fusion | flops 23592960 | bytes 62914824 | tf_op jit(solution)/shard_map/sub | solution.py:52
  771.5 0.0 copy-done.1
  (1 shorter events, 0.0 us)
Async XLA Ops:
  0.6 20.9 %copy-start = (bf16[1024,1024]{1,0:T(8,128)(2,1)S(1)}, bf16[1024,1024]{1,0:T(8,128)(2,1)}, u32[]{:S(2)}) copy-start(bf16[1024,1024]{1,0:T(8,128)(2,1)} %param.10) | copy-start | bytes 6291460
  0.6 15.1 %copy-start.3 = (bf16[40,40]{1,0:T(8,128)(2,1)S(1)}, bf16[40,40]{1,0:T(8,128)(2,1)}, u32[]{:S(2)}) copy-start(bf16[40,40]{1,0:T(8,128)(2,1)} %param.11) | copy-start | bytes 9604
  29.4 126.9 %copy-start.4 = (bf16[1024,1024]{1,0:T(8,128)(2,1)S(1)}, bf16[1024,1024]{1,0:T(8,128)(2,1)}, u32[]{:S(2)}) copy-start(bf16[1024,1024]{1,0:T(8,128)(2,1)} %param.9) | copy-start | bytes 6291460
  181.5 12.3 %copy-start.6 = (s32[64]{0:T(128)S(1)}, s32[64]{0:T(128)}, u32[]{:S(2)}) copy-start(s32[64]{0:T(128)} %param.8) | copy-start | bytes 772
  188.1 101.5 %all-to-all-start.1 = ((bf16[16,20,64,128]{3,2,1,0:T(8,128)(2,1)}), bf16[16,20,64,128]{3,2,1,0:T(8,128)(2,1)}, u32[]{:S(2)}, u32[]{:S(2)}) async-start(bf16[16,20,64,128]{3,2,1,0:T(8,128)(2,1)} %copy.32), calls=%async_computation.1 | async-start | bytes 10485760 | tf_op jit(solution)/shard_map/all_to_all | solution.py:46
  393.1 8.3 %copy-start.2 = (f32[64,40,1024]{2,1,0:T(8,128)}, f32[64,40,1024]{2,1,0:T(8,128)S(1)}, u32[]{:S(2)}) copy-start(f32[64,40,1024]{2,1,0:T(8,128)S(1)} %multiply_subtract_fusion.1) | copy-start | bytes 31457284
  402.9 122.3 %copy-start.5 = (bf16[1024,1024]{1,0:T(8,128)(2,1)S(1)}, bf16[1024,1024]{1,0:T(8,128)(2,1)}, u32[]{:S(2)}) copy-start(bf16[1024,1024]{1,0:T(8,128)(2,1)} %param.9) | copy-start | bytes 6291460
  747.6 23.9 %copy-start.1 = (bf16[1024,1024]{1,0:T(8,128)(2,1)S(1)}, bf16[1024,1024]{1,0:T(8,128)(2,1)}, u32[]{:S(2)}) copy-start(bf16[1024,1024]{1,0:T(8,128)(2,1)} %param.10) | copy-start | bytes 6291460

commit v2 on v1

v2 whole, which is shorter than its diff:
```python
import functools
import math

import jax
import jax.numpy as jnp
from jax import lax
from jax.experimental import pallas as pl
from jax.experimental.pallas import tpu as pltpu
from jax.sharding import PartitionSpec as P

ITERS = 2


noise_levels = (0.05, 0.2, 0.6, 1.5)


MESH = pl.DeviceIdType.MESH


def greet(devices, me):
    barrier = pltpu.get_barrier_semaphore()

    def signal(k, carry):
        pl.semaphore_signal(barrier, inc=1, device_id={"grid": lax.rem(me + k, devices)}, device_id_type=MESH)
        return carry

    lax.fori_loop(1, devices, signal, 0)
    pl.semaphore_wait(barrier, devices - 1)


def operator_kernel(
    mixed_ref, time_ref, station_ref, out_ref, pieces, held, result, out_send, out_recv, back_send, back_recv, own_out, own_back
):
    groups, devices, per, stations, lane = held.shape
    tiles = time_ref.shape[1] // lane
    group_variables = mixed_ref.shape[0] // groups
    me = lax.axis_index("grid")

    def outward(g, k, owner):
        peer = lax.rem(me + k, devices)
        return pltpu.make_async_remote_copy(
            src_ref=pieces.at[g, peer],
            dst_ref=held.at[g, owner],
            send_sem=out_send.at[g, k - 1],
            recv_sem=out_recv.at[g, k - 1],
            device_id={"grid": peer},
            device_id_type=MESH,
        )

    def homeward(g, k, owner):
        peer = lax.rem(me + k, devices)
        return pltpu.make_async_remote_copy(
            src_ref=result.at[g, peer],
            dst_ref=out_ref.at[g, owner],
            send_sem=back_send.at[g, k - 1],
            recv_sem=back_recv.at[g, k - 1],
            device_id={"grid": peer},
            device_id_type=MESH,
        )

    def stay_out(g):
        return pltpu.make_async_copy(pieces.at[g, me], held.at[g, me], own_out.at[g])

    def stay_back(g):
        return pltpu.make_async_copy(result.at[g, me], out_ref.at[g, me], own_back.at[g])

    def over(body):
        def step(k, carry):
            body(k, lax.rem(me + devices - k, devices))
            return carry

        lax.fori_loop(1, devices, step, 0)

    greet(devices, me)

    def send_group(g, carry):
        rows = mixed_ref[pl.ds(g * group_variables, group_variables)]
        rows = rows.reshape(group_variables * stations, tiles * lane)
        timed = jnp.dot(rows, time_ref[...], preferred_element_type=jnp.float32).astype(jnp.bfloat16)
        for v in range(group_variables):
            for tile in range(tiles):
                block = v * tiles + tile
                pieces[g, block // per, block % per] = timed[
                    v * stations : (v + 1) * stations, tile * lane : (tile + 1) * lane
                ]
        stay_out(g).start()
        over(lambda k, source: outward(g, k, me).start())
        return carry

    lax.fori_loop(0, groups, send_group, 0)

    def contract_group(g, carry):
        stay_out(g).wait()
        over(lambda k, source: outward(g, k, source).wait_recv())
        values = jnp.concatenate(
            [held[g, :, index].reshape(devices * stations, lane) for index in range(per)], axis=1
        )
        product = jnp.dot(station_ref[...], values, preferred_element_type=jnp.float32).astype(jnp.bfloat16)
        for index in range(per):
            result[g, :, index] = product[:, index * lane : (index + 1) * lane].reshape(devices, stations, lane)
        stay_back(g).start()
        over(lambda k, source: homeward(g, k, me).start())
        return carry

    lax.fori_loop(0, groups, contract_group, 0)

    def finish_group(g, carry):
        stay_back(g).wait()
        over(lambda k, source: homeward(g, k, source).wait_recv())
        over(lambda k, source: outward(g, k, source).wait_send())
        over(lambda k, source: homeward(g, k, source).wait_send())
        return carry

    lax.fori_loop(0, groups, finish_group, 0)


def apply_operator(mixed, time_kernel, station_kernel, devices, groups, per, lane):
    variables, stations, length = mixed.shape
    blocks = (groups, devices, per, stations, lane)
    remote = pltpu.SemaphoreType.DMA((groups, devices - 1))
    own = pltpu.SemaphoreType.DMA((groups,))
    return pl.pallas_call(
        operator_kernel,
        out_shape=jax.ShapeDtypeStruct(blocks, jnp.bfloat16),
        in_specs=[pl.BlockSpec(memory_space=pltpu.VMEM)] * 3,
        out_specs=pl.BlockSpec(memory_space=pl.ANY),
        scratch_shapes=[pltpu.VMEM(blocks, jnp.bfloat16)] * 3 + [remote] * 4 + [own] * 2,
        compiler_params=pltpu.CompilerParams(
            collective_id=0, has_side_effects=True, vmem_limit_bytes=48 * 2**20
        ),
        cost_estimate=pl.CostEstimate(
            flops=2 * variables * stations * length * (length + devices * stations),
            bytes_accessed=4 * variables * stations * length,
            transcendentals=0,
        ),
    )(mixed, time_kernel, station_kernel)


def total_kernel(devices, mine_ref, out_ref, held, send, recv):
    me = lax.axis_index("grid")

    def copy(k, owner):
        peer = lax.rem(me + k, devices)
        return pltpu.make_async_remote_copy(
            src_ref=mine_ref,
            dst_ref=held.at[owner],
            send_sem=send.at[k - 1],
            recv_sem=recv.at[k - 1],
            device_id={"grid": peer},
            device_id_type=MESH,
        )

    greet(devices, me)

    def start(k, carry):
        copy(k, me).start()
        return carry

    def end(k, carry):
        copy(k, lax.rem(me + devices - k, devices)).wait()
        return carry

    lax.fori_loop(1, devices, start, 0)
    held[me] = mine_ref[...]
    lax.fori_loop(1, devices, end, 0)
    out_ref[...] = jnp.sum(held[...], axis=0)


def grid_totals(first, second, devices):
    mine = jnp.where(lax.broadcasted_iota(jnp.int32, (8, 128), 0) == 0, first, second)
    sums = pl.pallas_call(
        functools.partial(total_kernel, devices),
        out_shape=jax.ShapeDtypeStruct((8, 128), jnp.float32),
        in_specs=[pl.BlockSpec(memory_space=pltpu.VMEM)],
        out_specs=pl.BlockSpec(memory_space=pltpu.VMEM),
        scratch_shapes=[
            pltpu.VMEM((devices, 8, 128), jnp.float32),
            pltpu.SemaphoreType.DMA((devices - 1,)),
            pltpu.SemaphoreType.DMA((devices - 1,)),
        ],
        compiler_params=pltpu.CompilerParams(collective_id=1, has_side_effects=True),
    )(mine)
    return sums[0, 0], sums[1, 0]


def body(observations, observation_mask, noise_class, station_kernel, time_kernel, variable_cov):
    devices = lax.axis_size("grid")
    stations, variables, length = observations.shape
    all_stations = station_kernel.shape[0]
    columns = variables * length // devices
    lane = math.gcd(math.gcd(128, columns), length)
    tiles = length // lane
    chunk = columns // lane
    groups = 5
    per = chunk // groups
    plain = lane < 128 or stations % 16 != 0 or chunk % groups != 0 or variables % groups != 0
    levels = jnp.zeros((stations,), jnp.float32)
    for level_index, level_value in enumerate(noise_levels):
        levels = levels + jnp.where(noise_class == level_index, level_value, 0.0)
    noise_cells = levels[:, None, None]
    mask_float = observation_mask.astype(jnp.float32)
    target = mask_float * observations
    solution = jnp.zeros_like(target)
    residual = target
    for inner_index in range(ITERS):
        rounded = residual.astype(jnp.bfloat16)
        mixed = jnp.einsum(
            "wv,svt->swt", variable_cov, rounded, preferred_element_type=jnp.float32
        ).astype(jnp.bfloat16)
        mixed = jnp.transpose(mixed, (1, 0, 2))
        if plain:
            timed = jnp.einsum(
                "wst,ut->wsu", mixed, time_kernel, preferred_element_type=jnp.float32
            ).astype(jnp.bfloat16)
            pieces = timed.reshape(variables, stations, tiles, lane)
            pieces = jnp.transpose(pieces, (0, 2, 1, 3)).reshape(devices, chunk, stations, lane)
            gathered = lax.all_to_all(pieces, "grid", split_axis=0, concat_axis=0, tiled=True)
            spaced = jnp.einsum(
                "arbs,bcsl->acrl",
                station_kernel.reshape(devices, stations, devices, stations),
                gathered,
                preferred_element_type=jnp.float32,
            ).astype(jnp.bfloat16)
            spaced = lax.all_to_all(spaced, "grid", split_axis=0, concat_axis=0, tiled=True)
        else:
            spaced = apply_operator(mixed, time_kernel, station_kernel, devices, groups, per, lane)
        spaced = jnp.transpose(spaced.reshape(variables, tiles, stations, lane), (0, 2, 1, 3))
        spaced = lax.optimization_barrier(spaced.reshape(variables, stations, length))
        spaced = lax.optimization_barrier(jnp.transpose(spaced, (1, 0, 2)))
        spaced = spaced.astype(jnp.float32)
        image = mask_float * spaced + noise_cells * residual
        norm_sq, curvature = jnp.sum(residual * residual), jnp.sum(residual * image)
        if plain:
            norm_sq, curvature = lax.psum((norm_sq, curvature), "grid")
        else:
            norm_sq, curvature = grid_totals(norm_sq, curvature, devices)
        step_size = norm_sq / curvature
        solution, residual = (solution + step_size * residual, residual - step_size * image)
    return (solution, residual)


def solution(mesh):
    return jax.shard_map(
        body,
        mesh=mesh,
        in_specs=(
            P(("parts", "grid"), None, None),
            P(("parts", "grid"), None, None),
            P(("parts", "grid")),
            P(),
            P(),
            P(),
        ),
        out_specs=(P(("parts", "grid"), None, None), P(("parts", "grid"), None, None)),
        check_vma=False,
    )
```

time: 780 us -> 624 us (0.80)
  Pallas kernels: 0 us -> 492 us
  blocking collectives: 447 us -> 0 us
  waiting for transfers between devices: 95.9 us -> 0 us
  local copies, waits for them, and re-layouts: 101 us -> 48.7 us
  matrix products: 35.3 us -> 7.77 us
  other arithmetic: 83.1 us -> 71.4 us
    pallas_call x0 -> x4, Pallas kernels: none -> 492 us  [the longest x2 458 us: apply_operator(): pl.pallas_call(operator_kernel, out_shape=jax.ShapeDtypeStruct(blocks, jn...]
    all_to_all x3 -> x0, blocking collectives: 360 us -> none  [the longest x2 240 us: body(): lax.all_to_all(pieces, 'grid', split_axis=0, concat_axis=0, tiled=True)]
    all_to_all x1 -> x0, waiting for transfers between devices: 95.9 us -> none  [body(): lax.all_to_all(spaced, 'grid', split_axis=0, concat_axis=0, tiled=True)]
    psum x2 -> x0, blocking collectives: 86.7 us -> none  [body(): lax.psum((jnp.sum(residual * residual), jnp.sum(residual * image)), 'grid')]
    convert_element_type x6 -> x0, local copies, waits for them, and re-layouts: 58.8 us -> none  [the longest x4 43.1 us: body(): spaced = spaced.reshape(stations, variables, length).astype(jnp.float32)]
    dot_general x4 -> x0, matrix products: 27.7 us -> none  [the longest x2 14.9 us: body(): jnp.einsum('rs,sk->rk', station_kernel, gathered, preferred_element_type=...]
    dot_general x0 -> x2, local copies, waits for them, and re-layouts: none -> 10.6 us  [body(): jnp.einsum('wv,svt->swt', variable_cov, rounded, preferred_element_type=j...]
    reshape x4 -> x2, local copies, waits for them, and re-layouts: 22.8 us -> 17.6 us  [body(): spaced.reshape(variables, stations, length)]
  transfers between devices with their start and end apart: 1 -> 0, of which waited for: 1 -> 0; matrix products, arithmetic and copies ran while one was open for 0% -> 0% of each run, Pallas kernels for 0% -> 0%
where the time goes in v2:
time: 624 us; the launch traced here: 623 us
  Pallas kernels  492 us (79%)
  other arithmetic  71.4 us (11%)
  local copies, waits for them, and re-layouts  48.7 us (8%)
  matrix products  7.77 us (1%)
    pallas_call x2, Pallas kernels, apply_operator(): pl.pallas_call(operator_kernel, out_shape=jax.ShapeDtypeStruct(blocks, jn...  458 us
    pallas_call x2, Pallas kernels, grid_totals(): pl.pallas_call(functools.partial(total_kernel, devices), out_shape=jax.Sh...  33.3 us
    sub x2, other arithmetic, body(): residual - step_size * image  32 us
    reduce_sum x2, other arithmetic, body(): jnp.sum(residual * residual)  21.2 us
    reshape x2, local copies, waits for them, and re-layouts, body(): spaced.reshape(variables, stations, length)  17.6 us
    transpose x2, local copies, waits for them, and re-layouts, body(): jnp.transpose(spaced.reshape(variables, tiles, stations, lane), (0, 2, 1,...  16.4 us
    mul x1, other arithmetic, body(): target = mask_float * observations  14.9 us

profile of v2, /device:TPU:0, one launch (start us, length us, event | category | flops | bytes accessed | tf_op | source)
XLA Modules:
  0.0 623.0 jit_solution(6202912707392197971)
XLA Ops:
  0.6 0.0 copy-start
  0.6 0.7 fusion.10
  1.3 14.9 %convert_multiply_fusion.2 = f32[64,40,1024]{2,1,0:T(8,128)} fusion(f32[64,40,1024]{2,1,0:T(8,128)} %param.6, s32[64,40,1024]{2,1,0:T(8,128)} %param.7), kind=kLoop, calls=%fused_computation.13 | loop fusion | flops 5242880 | bytes 31457280 | tf_op jit(solution)/shard_map/mul | solution.py:202
  16.2 0.0 copy-done
  16.2 0.0 copy-start.2
  16.2 0.0 copy-start.3
  16.2 5.9 fusion.4
  22.2 5.3 copy.18
  27.4 0.0 copy-done.2
  27.4 0.0 copy-done.3
  27.4 230.1 %shard_map.77 = bf16[5,16,4,64,128]{4,3,2,1,0:T(8,128)(2,1)} custom-call(bf16[40,64,1024]{2,1,0:T(8,128)(2,1)} %bitcast.33, bf16[1024,1024]{1,0:T(8,128)(2,1)S(1)} %copy-done.2, bf16[1024,1024]{1,0:T(8,128)(2,1)S(1)} %copy-done.3), custom_call_target="tpu_custom_call" | custom-call | flops 10737418240 | bytes 10485760 | tf_op jit(solution)/shard_map/pallas_call | solution.py:122
  257.5 8.2 %copy.9 = bf16[40,64,8,128]{3,2,0,1:T(8,128)(2,1)} copy(bf16[40,64,8,128]{3,1,2,0:T(8,128)(2,1)} %bitcast.34) | data formatting | bytes 10485760 | tf_op jit(solution)/shard_map/transpose | solution.py:227
  265.7 8.8 %reshape.20 = bf16[40,64,1024]{2,0,1:T(8,128)(2,1)} reshape(bf16[40,64,8,128]{3,2,0,1:T(8,128)(2,1)} %copy.9) | data formatting | bytes 10485760 | tf_op jit(solution)/shard_map/reshape | solution.py:228
  274.6 10.6 %multiply_reduce_fusion.3 = (f32[]{:T(128)}, f32[]{:T(128)}) fusion(f32[64,40,1024]{2,1,0:T(8,128)} %convert_multiply_fusion.2, f32[64]{0:T(128)S(1)} %fusion.10, bf16[64,40,1024]{2,1,0:T(8,128)(2,1)} %bitcast.31, s32[64,40,1024]{2,1,0:T(8,128)} %param.7), kind=kLoop, calls=%fused_computation.12 | loop fusion | flops 23592960 | bytes 26214664 | tf_op jit(solution)/shard_map/reduce_sum | solution.py:232
  285.2 1.3 compare_select_fusion.5
  286.4 0.7 iota.13.mine_ref
  287.1 16.7 %shard_map.78 = f32[8,128]{1,0:T(8,128)} custom-call(f32[8,128]{1,0:T(8,128)} %iota.13.mine_ref), custom_call_target="tpu_custom_call" | custom-call | tf_op jit(solution)/shard_map/pallas_call | solution.py:171
  303.8 1.3 fusion.12
  306.5 10.1 %multiply_subtract_fusion.1 = f32[64,40,1024]{2,1,0:T(8,128)S(1)} fusion(f32[64,40,1024]{2,1,0:T(8,128)} %convert_multiply_fusion.2, bf16[64,40,1024]{2,1,0:T(8,128)(2,1)} %bitcast.32, s32[64,40,1024]{2,1,0:T(8,128)} %param.7, f32[]{:T(128)} %bitcast.5, f32[64]{0:T(128)S(1)} %fusion.10), kind=kLoop, calls=%fused_computation.8 | loop fusion | flops 18350080 | bytes 36700420 | tf_op jit(solution)/shard_map/sub | solution.py:238
  316.6 0.0 copy-start.5
  316.6 0.0 copy-start.4
  316.6 1.8 fusion.2
  318.4 5.3 copy.19
  323.7 0.0 copy-done.5
  323.7 0.0 copy-done.4
  323.7 228.4 %shard_map.79 = bf16[5,16,4,64,128]{4,3,2,1,0:T(8,128)(2,1)} custom-call(bf16[40,64,1024]{2,1,0:T(8,128)(2,1)} %bitcast.35, bf16[1024,1024]{1,0:T(8,128)(2,1)S(1)} %copy-done.2, bf16[1024,1024]{1,0:T(8,128)(2,1)S(1)} %copy-done.4), custom_call_target="tpu_custom_call" | custom-call | flops 10737418240 | bytes 10485760 | tf_op jit(solution)/shard_map/pallas_call | solution.py:122
  552.1 8.2 %copy.11 = bf16[40,64,8,128]{3,2,0,1:T(8,128)(2,1)} copy(bf16[40,64,8,128]{3,1,2,0:T(8,128)(2,1)} %bitcast.36) | data formatting | bytes 10485760 | tf_op jit(solution)/shard_map/transpose | solution.py:227
  560.3 8.8 %reshape.22 = bf16[40,64,1024]{2,0,1:T(8,128)(2,1)} reshape(bf16[40,64,8,128]{3,2,0,1:T(8,128)(2,1)} %copy.11) | data formatting | bytes 10485760 | tf_op jit(solution)/shard_map/reshape | solution.py:228
  569.1 10.6 %multiply_reduce_fusion.1 = (f32[]{:T(128)}, f32[]{:T(128)}) fusion(f32[64,40,1024]{2,1,0:T(8,128)} %copy-done.5, f32[64]{0:T(128)S(1)} %fusion.10, bf16[64,40,1024]{2,1,0:T(8,128)(2,1)} %bitcast.29, s32[64,40,1024]{2,1,0:T(8,128)} %param.7), kind=kLoop, calls=%fused_computation.7 | loop fusion | flops 23592960 | bytes 26214664 | tf_op jit(solution)/shard_map/reduce_sum | solution.py:232
  579.7 1.3 compare_select_fusion.4
  581.0 0.7 iota.14.mine_ref
  581.7 16.6 %shard_map.80 = f32[8,128]{1,0:T(8,128)} custom-call(f32[8,128]{1,0:T(8,128)} %iota.14.mine_ref), custom_call_target="tpu_custom_call" | custom-call | tf_op jit(solution)/shard_map/pallas_call | solution.py:171
  598.3 1.3 fusion.11
  601.0 0.0 copy-start.1
  601.0 22.0 %multiply_subtract_fusion = (f32[64,40,1024]{2,1,0:T(8,128)}, f32[64,40,1024]{2,1,0:T(8,128)}) fusion(f32[64,40,1024]{2,1,0:T(8,128)} %copy-done.5, bf16[64,40,1024]{2,1,0:T(8,128)(2,1)} %bitcast.30, s32[64,40,1024]{2,1,0:T(8,128)} %param.7, f32[]{:T(128)} %bitcast.10, f32[64]{0:T(128)S(1)} %fusion.10, f32[64,40,1024]{2,1,0:T(8,128)} %convert_multiply_fusion.2, ...), kind=kLoop, calls=%fused_computation.2 | loop fusion | flops 26214400 | bytes 57671944 | tf_op jit(solution)/shard_map/sub | solution.py:238
  623.0 0.0 copy-done.1
Async XLA Ops:
  0.6 15.6 %copy-start = (bf16[40,40]{1,0:T(8,128)(2,1)S(1)}, bf16[40,40]{1,0:T(8,128)(2,1)}, u32[]{:S(2)}) copy-start(bf16[40,40]{1,0:T(8,128)(2,1)} %param.11) | copy-start | bytes 9604
  16.2 11.2 %copy-start.2 = (bf16[1024,1024]{1,0:T(8,128)(2,1)S(1)}, bf16[1024,1024]{1,0:T(8,128)(2,1)}, u32[]{:S(2)}) copy-start(bf16[1024,1024]{1,0:T(8,128)(2,1)} %time_ref.3) | copy-start | bytes 6291460
  16.2 11.2 %copy-start.3 = (bf16[1024,1024]{1,0:T(8,128)(2,1)S(1)}, bf16[1024,1024]{1,0:T(8,128)(2,1)}, u32[]{:S(2)}) copy-start(bf16[1024,1024]{1,0:T(8,128)(2,1)} %station_ref.3) | copy-start | bytes 6291460
  316.6 7.1 %copy-start.5 = (f32[64,40,1024]{2,1,0:T(8,128)}, f32[64,40,1024]{2,1,0:T(8,128)S(1)}, u32[]{:S(2)}) copy-start(f32[64,40,1024]{2,1,0:T(8,128)S(1)} %multiply_subtract_fusion.1) | copy-start | bytes 31457284
  316.6 7.1 %copy-start.4 = (bf16[1024,1024]{1,0:T(8,128)(2,1)S(1)}, bf16[1024,1024]{1,0:T(8,128)(2,1)}, u32[]{:S(2)}) copy-start(bf16[1024,1024]{1,0:T(8,128)(2,1)} %station_ref.3) | copy-start | bytes 6291460
  601.0 22.0 %copy-start.1 = (bf16[40,40]{1,0:T(8,128)(2,1)S(1)}, bf16[40,40]{1,0:T(8,128)(2,1)}, u32[]{:S(2)}) copy-start(bf16[40,40]{1,0:T(8,128)(2,1)} %param.11) | copy-start | bytes 9604

commit v3 on v2

--- a/solution.py
+++ b/solution.py
@@ -5,6 +5,7 @@
 import jax.numpy as jnp
 from jax import lax
 from jax.experimental import pallas as pl
+from jax.experimental.layout import Layout, with_layout_constraint
 from jax.experimental.pallas import tpu as pltpu
 from jax.sharding import PartitionSpec as P
 
@@ -31,8 +32,8 @@
 def operator_kernel(
     mixed_ref, time_ref, station_ref, out_ref, pieces, held, result, out_send, out_recv, back_send, back_recv, own_out, own_back
 ):
-    groups, devices, per, stations, lane = held.shape
-    tiles = time_ref.shape[1] // lane
+    groups, devices, stations, width = held.shape
+    spans = time_ref.shape[1] // width
     group_variables = mixed_ref.shape[0] // groups
     me = lax.axis_index("grid")
 
@@ -47,11 +48,16 @@
             device_id_type=MESH,
         )
 
+    def place(g, owner):
+        variable = g * group_variables + owner // spans
+        start = pl.multiple_of(lax.rem(owner, spans) * width, width)
+        return out_ref.at[variable, :, pl.ds(start, width)]
+
     def homeward(g, k, owner):
         peer = lax.rem(me + k, devices)
         return pltpu.make_async_remote_copy(
             src_ref=result.at[g, peer],
-            dst_ref=out_ref.at[g, owner],
+            dst_ref=place(g, owner),
             send_sem=back_send.at[g, k - 1],
             recv_sem=back_recv.at[g, k - 1],
             device_id={"grid": peer},
@@ -62,7 +68,7 @@
         return pltpu.make_async_copy(pieces.at[g, me], held.at[g, me], own_out.at[g])
 
     def stay_back(g):
-        return pltpu.make_async_copy(result.at[g, me], out_ref.at[g, me], own_back.at[g])
+        return pltpu.make_async_copy(result.at[g, me], place(g, me), own_back.at[g])
 
     def over(body):
         def step(k, carry):
@@ -75,13 +81,12 @@
 
     def send_group(g, carry):
         rows = mixed_ref[pl.ds(g * group_variables, group_variables)]
-        rows = rows.reshape(group_variables * stations, tiles * lane)
+        rows = rows.reshape(group_variables * stations, spans * width)
         timed = jnp.dot(rows, time_ref[...], preferred_element_type=jnp.float32).astype(jnp.bfloat16)
         for v in range(group_variables):
-            for tile in range(tiles):
-                block = v * tiles + tile
-                pieces[g, block // per, block % per] = timed[
-                    v * stations : (v + 1) * stations, tile * lane : (tile + 1) * lane
+            for span in range(spans):
+                pieces[g, v * spans + span] = timed[
+                    v * stations : (v + 1) * stations, span * width : (span + 1) * width
                 ]
         stay_out(g).start()
         over(lambda k, source: outward(g, k, me).start())
@@ -92,12 +97,9 @@
     def contract_group(g, carry):
         stay_out(g).wait()
         over(lambda k, source: outward(g, k, source).wait_recv())
-        values = jnp.concatenate(
-            [held[g, :, index].reshape(devices * stations, lane) for index in range(per)], axis=1
-        )
+        values = held[g].reshape(devices * stations, width)
         product = jnp.dot(station_ref[...], values, preferred_element_type=jnp.float32).astype(jnp.bfloat16)
-        for index in range(per):
-            result[g, :, index] = product[:, index * lane : (index + 1) * lane].reshape(devices, stations, lane)
+        result[g] = product.reshape(devices, stations, width)
         stay_back(g).start()
         over(lambda k, source: homeward(g, k, me).start())
         return carry
@@ -114,19 +116,19 @@
     lax.fori_loop(0, groups, finish_group, 0)
 
 
-def apply_operator(mixed, time_kernel, station_kernel, devices, groups, per, lane):
+def apply_operator(mixed, time_kernel, station_kernel, devices, groups, width):
     variables, stations, length = mixed.shape
-    blocks = (groups, devices, per, stations, lane)
+    blocks = (groups, devices, stations, width)
     remote = pltpu.SemaphoreType.DMA((groups, devices - 1))
     own = pltpu.SemaphoreType.DMA((groups,))
     return pl.pallas_call(
         operator_kernel,
-        out_shape=jax.ShapeDtypeStruct(blocks, jnp.bfloat16),
+        out_shape=jax.ShapeDtypeStruct(mixed.shape, jnp.bfloat16),
         in_specs=[pl.BlockSpec(memory_space=pltpu.VMEM)] * 3,
         out_specs=pl.BlockSpec(memory_space=pl.ANY),
         scratch_shapes=[pltpu.VMEM(blocks, jnp.bfloat16)] * 3 + [remote] * 4 + [own] * 2,
         compiler_params=pltpu.CompilerParams(
-            collective_id=0, has_side_effects=True, vmem_limit_bytes=48 * 2**20
+            collective_id=0, has_side_effects=True, vmem_limit_bytes=40 * 2**20
         ),
         cost_estimate=pl.CostEstimate(
             flops=2 * variables * stations * length * (length + devices * stations),
@@ -192,8 +194,8 @@
     tiles = length // lane
     chunk = columns // lane
     groups = 5
-    per = chunk // groups
-    plain = lane < 128 or stations % 16 != 0 or chunk % groups != 0 or variables % groups != 0
+    per = max(chunk // groups, 1)
+    plain = lane < 128 or stations % 16 != 0 or variables % groups != 0 or chunk % groups != 0 or tiles % per != 0
     levels = jnp.zeros((stations,), jnp.float32)
     for level_index, level_value in enumerate(noise_levels):
         levels = levels + jnp.where(noise_class == level_index, level_value, 0.0)
@@ -222,14 +224,15 @@
                 preferred_element_type=jnp.float32,
             ).astype(jnp.bfloat16)
             spaced = lax.all_to_all(spaced, "grid", split_axis=0, concat_axis=0, tiled=True)
+            spaced = jnp.transpose(spaced.reshape(variables, tiles, stations, lane), (0, 2, 1, 3))
+            spaced = spaced.reshape(variables, stations, length)
         else:
-            spaced = apply_operator(mixed, time_kernel, station_kernel, devices, groups, per, lane)
-        spaced = jnp.transpose(spaced.reshape(variables, tiles, stations, lane), (0, 2, 1, 3))
-        spaced = lax.optimization_barrier(spaced.reshape(variables, stations, length))
-        spaced = lax.optimization_barrier(jnp.transpose(spaced, (1, 0, 2)))
+            spaced = apply_operator(mixed, time_kernel, station_kernel, devices, groups, per * lane)
+        spaced = with_layout_constraint(jnp.transpose(spaced, (1, 0, 2)), Layout((0, 1, 2)))
         spaced = spaced.astype(jnp.float32)
         image = mask_float * spaced + noise_cells * residual
-        norm_sq, curvature = jnp.sum(residual * residual), jnp.sum(residual * image)
+        norm_sq = jnp.sum(residual * residual)
+        curvature = jnp.sum(residual * (spaced + noise_cells * residual))
         if plain:
             norm_sq, curvature = lax.psum((norm_sq, curvature), "grid")
         else:

time: 624 us -> 597 us (0.957)
  local copies, waits for them, and re-layouts: 48.7 us -> 19.2 us
    reshape x2 -> x0, local copies, waits for them, and re-layouts: 17.6 us -> none  [body(): spaced.reshape(variables, stations, length)]
    transpose x2 -> x0, local copies, waits for them, and re-layouts: 16.4 us -> none  [body(): jnp.transpose(spaced.reshape(variables, tiles, stations, lane), (0, 2, 1,...]
where the time goes in v3:
time: 597 us
  Pallas kernels  492 us (82%)
  other arithmetic  74.2 us (12%)
  local copies, waits for them, and re-layouts  19.2 us (3%)
  matrix products  7.79 us (1%)
    pallas_call x2, Pallas kernels, apply_operator(): pl.pallas_call(operator_kernel, out_shape=jax.ShapeDtypeStruct(mixed.shap...  458 us
    pallas_call x2, Pallas kernels, grid_totals(): pl.pallas_call(functools.partial(total_kernel, devices), out_shape=jax.Sh...  33.3 us
    sub x2, other arithmetic, body(): residual - step_size * image  30.1 us
    reduce_sum x2, other arithmetic, body(): norm_sq = jnp.sum(residual * residual)  26 us
    mul x1, other arithmetic, body(): target = mask_float * observations  14.9 us

profile of v3, /device:TPU:0, one launch (start us, length us, event | category | flops | bytes accessed | tf_op | source)
XLA Modules:
  0.0 596.6 jit_solution(16473732935780021118)
XLA Ops:
  0.6 0.0 copy-start
  0.6 0.7 fusion.20
  1.3 14.9 %convert_multiply_fusion.2 = f32[64,40,1024]{2,1,0:T(8,128)} fusion(f32[64,40,1024]{2,1,0:T(8,128)} %param.6, s32[64,40,1024]{2,1,0:T(8,128)} %param.7), kind=kLoop, calls=%fused_computation.19 | loop fusion | flops 5242880 | bytes 31457280 | tf_op jit(solution)/shard_map/mul | solution.py:204
  16.2 0.0 copy-done
  16.2 0.0 copy-start.4
  16.2 0.0 copy-start.5
  16.2 5.9 fusion.14
  22.2 0.0 slice-start
  22.2 5.3 copy.22
  27.5 0.0 copy-done.4
  27.5 0.0 copy-done.5
  27.5 0.0 slice-start.1
  27.5 0.0 slice-start.2
  27.5 230.1 %shard_map.77 = bf16[40,64,1024]{2,1,0:T(8,128)(2,1)S(1)} custom-call(bf16[40,64,1024]{2,1,0:T(8,128)(2,1)} %bitcast.21, bf16[1024,1024]{1,0:T(8,128)(2,1)S(1)} %copy-done.4, bf16[1024,1024]{1,0:T(8,128)(2,1)S(1)} %copy-done.5), custom_call_target="tpu_custom_call" | custom-call | flops 10737418240 | bytes 10485760 | tf_op jit(solution)/shard_map/pallas_call | solution.py:124
  257.6 0.0 copy-start.3
  257.6 2.3 copy-done.3
  260.0 0.0 slice-done
  260.0 0.0 slice-done.1
  260.0 0.0 slice-done.2
  260.0 13.0 %multiply_reduce_fusion.1 = (f32[]{:T(128)}, f32[]{:T(128)}) fusion(f32[64,40,1024]{2,1,0:T(8,128)S(1)} %bitcast.20, f32[64]{0:T(128)S(1)} %fusion.20, bf16[40,64,1024]{2,1,0:T(8,128)(2,1)S(1)} %shard_map.77), kind=kLoop, calls=%fused_computation.18 | loop fusion | flops 18350078 | bytes 15728904 | tf_op jit(solution)/shard_map/reduce_sum | solution.py:234
  273.0 1.2 compare_select_fusion.5
  274.2 0.7 iota.13.mine_ref
  274.9 16.7 %shard_map.78 = f32[8,128]{1,0:T(8,128)} custom-call(f32[8,128]{1,0:T(8,128)} %iota.13.mine_ref), custom_call_target="tpu_custom_call" | custom-call | tf_op jit(solution)/shard_map/pallas_call | solution.py:173
  291.6 1.3 fusion.22
  294.3 10.4 %fusion.4 = f32[64,40,1024]{2,1,0:T(8,128)S(1)} fusion(f32[64,40,1024]{2,1,0:T(8,128)} %convert_multiply_fusion.2, s32[64,40,1024]{2,1,0:T(8,128)} %param.7, f32[]{:T(128)} %bitcast.3, f32[64]{0:T(128)S(1)} %fusion.20, bf16[40,64,1024]{2,1,0:T(8,128)(2,1)} %copy-done.3), kind=kLoop, calls=%fused_computation.8 | loop fusion | flops 18350080 | bytes 36700420 | tf_op jit(solution)/shard_map/sub | solution.py:241
  304.7 0.0 copy-start.7
  304.7 0.0 copy-start.6
  304.7 1.8 fusion.12
  306.6 5.2 copy.23
  311.8 0.0 copy-done.6
  311.8 228.3 %shard_map.79 = bf16[40,64,1024]{2,1,0:T(8,128)(2,1)S(1)} custom-call(bf16[40,64,1024]{2,1,0:T(8,128)(2,1)} %bitcast.22, bf16[1024,1024]{1,0:T(8,128)(2,1)S(1)} %copy-done.4, bf16[1024,1024]{1,0:T(8,128)(2,1)S(1)} %copy-done.6), custom_call_target="tpu_custom_call" | custom-call | flops 10737418240 | bytes 10485760 | tf_op jit(solution)/shard_map/pallas_call | solution.py:124
  540.1 0.0 copy-done.7
  540.1 0.0 copy-start.2
  540.1 2.3 copy-done.2
  542.4 13.0 %multiply_reduce_fusion = (f32[]{:T(128)}, f32[]{:T(128)}) fusion(f32[64,40,1024]{2,1,0:T(8,128)S(1)} %fusion.4, f32[64]{0:T(128)S(1)} %fusion.20, bf16[40,64,1024]{2,1,0:T(8,128)(2,1)S(1)} %shard_map.79), kind=kLoop, calls=%fused_computation.17 | loop fusion | flops 18350078 | bytes 15728904 | tf_op jit(solution)/shard_map/reduce_sum | solution.py:234
  555.4 1.3 compare_select_fusion.4
  556.7 0.7 iota.14.mine_ref
  557.3 16.6 %shard_map.80 = f32[8,128]{1,0:T(8,128)} custom-call(f32[8,128]{1,0:T(8,128)} %iota.14.mine_ref), custom_call_target="tpu_custom_call" | custom-call | tf_op jit(solution)/shard_map/pallas_call | solution.py:173
  574.0 1.3 fusion.21
  576.7 0.0 copy-start.1
  576.7 19.7 %fusion.9 = (f32[64,40,1024]{2,1,0:T(8,128)}, f32[64,40,1024]{2,1,0:T(8,128)}) fusion(f32[64,40,1024]{2,1,0:T(8,128)} %copy-done.7, s32[64,40,1024]{2,1,0:T(8,128)} %param.7, f32[]{:T(128)} %bitcast.6, f32[64]{0:T(128)S(1)} %fusion.20, bf16[40,64,1024]{2,1,0:T(8,128)(2,1)} %copy-done.2, f32[64,40,1024]{2,1,0:T(8,128)} %convert_multiply_fusion.2, f32[]{:T(128)} %bitcast.3), kind=kLoop, calls=%fused_computation.13 | loop fusion | flops 26214400 | bytes 57671944 | tf_op jit(solution)/shard_map/sub | solution.py:241
  596.4 0.0 copy-done.1
  (1 shorter events, 0.0 us)
Async XLA Ops:
  0.6 15.6 %copy-start = (bf16[40,40]{1,0:T(8,128)(2,1)S(1)}, bf16[40,40]{1,0:T(8,128)(2,1)}, u32[]{:S(2)}) copy-start(bf16[40,40]{1,0:T(8,128)(2,1)} %param.11) | copy-start | bytes 9604
  16.2 11.2 %copy-start.4 = (bf16[1024,1024]{1,0:T(8,128)(2,1)S(1)}, bf16[1024,1024]{1,0:T(8,128)(2,1)}, u32[]{:S(2)}) copy-start(bf16[1024,1024]{1,0:T(8,128)(2,1)} %time_ref.3) | copy-start | bytes 6291460
  16.2 11.2 %copy-start.5 = (bf16[1024,1024]{1,0:T(8,128)(2,1)S(1)}, bf16[1024,1024]{1,0:T(8,128)(2,1)}, u32[]{:S(2)}) copy-start(bf16[1024,1024]{1,0:T(8,128)(2,1)} %station_ref.3) | copy-start | bytes 6291460
  22.2 237.8 %slice-start = ((s8[10485760]{0:T(1024)(128)(4,1)}), s8[4194304]{0:T(1024)(128)(4,1)S(1)}, s32[]{:S(2)}) async-start(s8[10485760]{0:T(1024)(128)(4,1)} %bitcast.19), calls=%async_computation | async-start | bytes 8388608
  27.5 232.5 %slice-start.1 = ((s8[10485760]{0:T(1024)(128)(4,1)}), s8[4194304]{0:T(1024)(128)(4,1)S(1)}, s32[]{:S(2)}) async-start(s8[10485760]{0:T(1024)(128)(4,1)} %bitcast.19), calls=%async_computation.1 | async-start | bytes 8388608
  27.5 232.5 %slice-start.2 = ((s8[10485760]{0:T(1024)(128)(4,1)}), s8[2097152]{0:T(1024)(128)(4,1)S(1)}, s32[]{:S(2)}) async-start(s8[10485760]{0:T(1024)(128)(4,1)} %bitcast.19), calls=%async_computation.2 | async-start | bytes 4194304
  257.6 2.4 copy-start.3
  304.7 235.4 %copy-start.7 = (f32[64,40,1024]{2,1,0:T(8,128)}, f32[64,40,1024]{2,1,0:T(8,128)S(1)}, u32[]{:S(2)}) copy-start(f32[64,40,1024]{2,1,0:T(8,128)S(1)} %fusion.4) | copy-start | bytes 31457284
  304.7 7.1 %copy-start.6 = (bf16[1024,1024]{1,0:T(8,128)(2,1)S(1)}, bf16[1024,1024]{1,0:T(8,128)(2,1)}, u32[]{:S(2)}) copy-start(bf16[1024,1024]{1,0:T(8,128)(2,1)} %station_ref.3) | copy-start | bytes 6291460
  540.1 2.3 copy-start.2
  576.7 19.7 %copy-start.1 = (bf16[40,40]{1,0:T(8,128)(2,1)S(1)}, bf16[40,40]{1,0:T(8,128)(2,1)}, u32[]{:S(2)}) copy-start(bf16[40,40]{1,0:T(8,128)(2,1)} %param.11) | copy-start | bytes 9604

commit v4 on v3

--- a/solution.py
+++ b/solution.py
@@ -193,7 +193,7 @@
     lane = math.gcd(math.gcd(128, columns), length)
     tiles = length // lane
     chunk = columns // lane
-    groups = 5
+    groups = 10
     per = max(chunk // groups, 1)
     plain = lane < 128 or stations % 16 != 0 or variables % groups != 0 or chunk % groups != 0 or tiles % per != 0
     levels = jnp.zeros((stations,), jnp.float32)

time: 597 us -> 601 us (level)
    pallas_call x2, Pallas kernels: 458 us -> 473 us  [apply_operator(): pl.pallas_call(operator_kernel, out_shape=jax.ShapeDtypeStruct(mixed.shap...]
    pallas_call x2, Pallas kernels: 33.3 us -> 22.5 us  [grid_totals(): pl.pallas_call(functools.partial(total_kernel, devices), out_shape=jax.Sh...]
where the time goes in v4:
time: 601 us
  Pallas kernels  496 us (83%)
  other arithmetic  74.2 us (12%)
  local copies, waits for them, and re-layouts  19.2 us (3%)
  matrix products  7.79 us (1%)
    pallas_call x2, Pallas kernels, apply_operator(): pl.pallas_call(operator_kernel, out_shape=jax.ShapeDtypeStruct(mixed.shap...  473 us
    sub x2, other arithmetic, body(): residual - step_size * image  30.1 us
    reduce_sum x2, other arithmetic, body(): norm_sq = jnp.sum(residual * residual)  26 us
    pallas_call x2, Pallas kernels, grid_totals(): pl.pallas_call(functools.partial(total_kernel, devices), out_shape=jax.Sh...  22.5 us
    mul x1, other arithmetic, body(): target = mask_float * observations  14.9 us

profile of v4, /device:TPU:0, one launch (start us, length us, event | category | flops | bytes accessed | tf_op | source)
XLA Modules:
  0.0 600.6 jit_solution(4394034075746333141)
XLA Ops:
  0.6 0.0 copy-start
  0.6 0.7 fusion.20
  1.3 14.9 %convert_multiply_fusion.2 = f32[64,40,1024]{2,1,0:T(8,128)} fusion(f32[64,40,1024]{2,1,0:T(8,128)} %param.6, s32[64,40,1024]{2,1,0:T(8,128)} %param.7), kind=kLoop, calls=%fused_computation.19 | loop fusion | flops 5242880 | bytes 31457280 | tf_op jit(solution)/shard_map/mul | solution.py:204
  16.2 0.0 copy-done
  16.2 0.0 copy-start.4
  16.2 0.0 copy-start.5
  16.2 5.9 fusion.14
  22.2 0.0 slice-start
  22.2 5.3 copy.22
  27.5 0.0 copy-done.4
  27.5 0.0 copy-done.5
  27.5 0.0 slice-start.1
  27.5 0.0 slice-start.2
  27.5 237.6 %shard_map.77 = bf16[40,64,1024]{2,1,0:T(8,128)(2,1)S(1)} custom-call(bf16[40,64,1024]{2,1,0:T(8,128)(2,1)} %bitcast.21, bf16[1024,1024]{1,0:T(8,128)(2,1)S(1)} %copy-done.4, bf16[1024,1024]{1,0:T(8,128)(2,1)S(1)} %copy-done.5), custom_call_target="tpu_custom_call" | custom-call | flops 10737418240 | bytes 10485760 | tf_op jit(solution)/shard_map/pallas_call | solution.py:124
  265.0 0.0 copy-start.3
  265.0 2.3 copy-done.3
  267.4 0.0 slice-done
  267.4 0.0 slice-done.1
  267.4 0.0 slice-done.2
  267.4 13.0 %multiply_reduce_fusion.1 = (f32[]{:T(128)}, f32[]{:T(128)}) fusion(f32[64,40,1024]{2,1,0:T(8,128)S(1)} %bitcast.20, f32[64]{0:T(128)S(1)} %fusion.20, bf16[40,64,1024]{2,1,0:T(8,128)(2,1)S(1)} %shard_map.77), kind=kLoop, calls=%fused_computation.18 | loop fusion | flops 18350078 | bytes 15728904 | tf_op jit(solution)/shard_map/reduce_sum | solution.py:234
  280.4 1.2 compare_select_fusion.5
  281.6 0.7 iota.13.mine_ref
  282.3 11.3 %shard_map.78 = f32[8,128]{1,0:T(8,128)} custom-call(f32[8,128]{1,0:T(8,128)} %iota.13.mine_ref), custom_call_target="tpu_custom_call" | custom-call | tf_op jit(solution)/shard_map/pallas_call | solution.py:173
  293.6 1.3 fusion.22
  296.3 10.4 %fusion.4 = f32[64,40,1024]{2,1,0:T(8,128)S(1)} fusion(f32[64,40,1024]{2,1,0:T(8,128)} %convert_multiply_fusion.2, s32[64,40,1024]{2,1,0:T(8,128)} %param.7, f32[]{:T(128)} %bitcast.3, f32[64]{0:T(128)S(1)} %fusion.20, bf16[40,64,1024]{2,1,0:T(8,128)(2,1)} %copy-done.3), kind=kLoop, calls=%fused_computation.8 | loop fusion | flops 18350080 | bytes 36700420 | tf_op jit(solution)/shard_map/sub | solution.py:241
  306.7 0.0 copy-start.7
  306.7 0.0 copy-start.6
  306.7 1.8 fusion.12
  308.6 5.2 copy.23
  313.8 0.0 copy-done.6
  313.8 235.6 %shard_map.79 = bf16[40,64,1024]{2,1,0:T(8,128)(2,1)S(1)} custom-call(bf16[40,64,1024]{2,1,0:T(8,128)(2,1)} %bitcast.22, bf16[1024,1024]{1,0:T(8,128)(2,1)S(1)} %copy-done.4, bf16[1024,1024]{1,0:T(8,128)(2,1)S(1)} %copy-done.6), custom_call_target="tpu_custom_call" | custom-call | flops 10737418240 | bytes 10485760 | tf_op jit(solution)/shard_map/pallas_call | solution.py:124
  549.5 0.0 copy-done.7
  549.5 0.0 copy-start.2
  549.5 2.3 copy-done.2
  551.8 13.0 %multiply_reduce_fusion = (f32[]{:T(128)}, f32[]{:T(128)}) fusion(f32[64,40,1024]{2,1,0:T(8,128)S(1)} %fusion.4, f32[64]{0:T(128)S(1)} %fusion.20, bf16[40,64,1024]{2,1,0:T(8,128)(2,1)S(1)} %shard_map.79), kind=kLoop, calls=%fused_computation.17 | loop fusion | flops 18350078 | bytes 15728904 | tf_op jit(solution)/shard_map/reduce_sum | solution.py:234
  564.8 1.3 compare_select_fusion.4
  566.0 0.7 iota.14.mine_ref
  566.7 11.2 %shard_map.80 = f32[8,128]{1,0:T(8,128)} custom-call(f32[8,128]{1,0:T(8,128)} %iota.14.mine_ref), custom_call_target="tpu_custom_call" | custom-call | tf_op jit(solution)/shard_map/pallas_call | solution.py:173
  577.9 1.3 fusion.21
  580.7 0.0 copy-start.1
  580.7 19.7 %fusion.9 = (f32[64,40,1024]{2,1,0:T(8,128)}, f32[64,40,1024]{2,1,0:T(8,128)}) fusion(f32[64,40,1024]{2,1,0:T(8,128)} %copy-done.7, s32[64,40,1024]{2,1,0:T(8,128)} %param.7, f32[]{:T(128)} %bitcast.6, f32[64]{0:T(128)S(1)} %fusion.20, bf16[40,64,1024]{2,1,0:T(8,128)(2,1)} %copy-done.2, f32[64,40,1024]{2,1,0:T(8,128)} %convert_multiply_fusion.2, f32[]{:T(128)} %bitcast.3), kind=kLoop, calls=%fused_computation.13 | loop fusion | flops 26214400 | bytes 57671944 | tf_op jit(solution)/shard_map/sub | solution.py:241
  600.4 0.0 copy-done.1
  (1 shorter events, 0.0 us)
Async XLA Ops:
  0.6 15.6 %copy-start = (bf16[40,40]{1,0:T(8,128)(2,1)S(1)}, bf16[40,40]{1,0:T(8,128)(2,1)}, u32[]{:S(2)}) copy-start(bf16[40,40]{1,0:T(8,128)(2,1)} %param.11) | copy-start | bytes 9604
  16.2 11.2 %copy-start.4 = (bf16[1024,1024]{1,0:T(8,128)(2,1)S(1)}, bf16[1024,1024]{1,0:T(8,128)(2,1)}, u32[]{:S(2)}) copy-start(bf16[1024,1024]{1,0:T(8,128)(2,1)} %time_ref.3) | copy-start | bytes 6291460
  16.2 11.2 %copy-start.5 = (bf16[1024,1024]{1,0:T(8,128)(2,1)S(1)}, bf16[1024,1024]{1,0:T(8,128)(2,1)}, u32[]{:S(2)}) copy-start(bf16[1024,1024]{1,0:T(8,128)(2,1)} %station_ref.3) | copy-start | bytes 6291460
  22.2 245.2 %slice-start = ((s8[10485760]{0:T(1024)(128)(4,1)}), s8[4194304]{0:T(1024)(128)(4,1)S(1)}, s32[]{:S(2)}) async-start(s8[10485760]{0:T(1024)(128)(4,1)} %bitcast.19), calls=%async_computation | async-start | bytes 8388608
  27.5 239.9 %slice-start.1 = ((s8[10485760]{0:T(1024)(128)(4,1)}), s8[4194304]{0:T(1024)(128)(4,1)S(1)}, s32[]{:S(2)}) async-start(s8[10485760]{0:T(1024)(128)(4,1)} %bitcast.19), calls=%async_computation.1 | async-start | bytes 8388608
  27.5 239.9 %slice-start.2 = ((s8[10485760]{0:T(1024)(128)(4,1)}), s8[2097152]{0:T(1024)(128)(4,1)S(1)}, s32[]{:S(2)}) async-start(s8[10485760]{0:T(1024)(128)(4,1)} %bitcast.19), calls=%async_computation.2 | async-start | bytes 4194304
  265.0 2.4 copy-start.3
  306.7 242.7 %copy-start.7 = (f32[64,40,1024]{2,1,0:T(8,128)}, f32[64,40,1024]{2,1,0:T(8,128)S(1)}, u32[]{:S(2)}) copy-start(f32[64,40,1024]{2,1,0:T(8,128)S(1)} %fusion.4) | copy-start | bytes 31457284
  306.7 7.1 %copy-start.6 = (bf16[1024,1024]{1,0:T(8,128)(2,1)S(1)}, bf16[1024,1024]{1,0:T(8,128)(2,1)}, u32[]{:S(2)}) copy-start(bf16[1024,1024]{1,0:T(8,128)(2,1)} %station_ref.3) | copy-start | bytes 6291460
  549.5 2.3 copy-start.2
  580.7 19.7 %copy-start.1 = (bf16[40,40]{1,0:T(8,128)(2,1)S(1)}, bf16[40,40]{1,0:T(8,128)(2,1)}, u32[]{:S(2)}) copy-start(bf16[40,40]{1,0:T(8,128)(2,1)} %param.11) | copy-start | bytes 9604
